TPU v7x, 512 devices: a whole 4x8x8 slice. The times are simulated.
512 devices in a mesh: lists: 64 (over x, y, core), qb: 8 (over z).
Axes of the slice: x: 4, y: 8, z: 8, core: 2. Of those that a mesh axis runs over, the one named last changes fastest.
Arguments:
- queries: float32 [16384, 128], P(('lists', 'qb')), may hold values from -28 to 28
- reader_logits: float32 [16384, 16], P(('lists', 'qb')), may hold values from -8 to 8
- probe_shards: int32 [16384, 16], P(('lists', 'qb')), may hold values from 0 to 63, all different within a row; in each aligned block of 32 rows (0 to 31, 32 to 63, ...) at most 16 rows name the same one
- probe_within: int32 [16384, 16], P(('lists', 'qb')), may hold values from 0 to 7
- passages: float32 [49152, 128], P('lists'), may hold values from -6 to 6
- list_sizes: int32 [64, 8], P('lists'), may hold values from 1 to 192, 768 in all within a row
Outputs:
- query_grad: float32 [16384, 128], P(('lists', 'qb'))
- passage_grad: float32 [49152, 128], P(('lists', 'qb'))
- query_loss: float32 [16384], P(('lists', 'qb'))
Inputs may be any that keep to these rules, and one draw needn't show every extreme that they name: `probe_shards`: each row names 16 different values. Among the rows of one device no value is named by more than 16 rows, a bound that some block reaches. `list_sizes`: each row sums to 768, and its largest entry is 192.
All inputs are finite; a program needn't handle non-finite values.
Results may differ from a plain program's by a relative error of at most 0.0003.
Values sent between devices are 32-bit elements; how exact they have to be, the bound alone decides.
A program may use at most 64 MiB of HBM per device.

v0:
```python
import math

import jax
import jax.numpy as jnp
from jax import lax
from jax.sharding import PartitionSpec as P


def left_product(table, values):
    return lax.dot_general(
        table,
        values,
        (((0,), (0,)), ((), ())),
        precision=lax.Precision.HIGHEST,
        preferred_element_type=jnp.float32,
    )


def right_product(table, values):
    return jnp.dot(
        table, values, precision=lax.Precision.HIGHEST, preferred_element_type=jnp.float32
    )


def local(queries, reader_logits, probe_shards, probe_within, passages, list_sizes):
    per_dev, emb_width = queries.shape
    probes = probe_shards.shape[1]
    shards = lax.axis_size("lists")
    capacity = min(per_dev, 2 * per_dev * probes // shards)
    score_scale = 1.0 / math.sqrt(emb_width)
    slot_total = shards * capacity
    probe_count = per_dev * probes
    target_shard = probe_shards.reshape(-1)
    within = probe_within.reshape(-1)
    shard_hot = (target_shard[:, None] == jnp.arange(shards, dtype=jnp.int32)[None, :]).astype(
        jnp.float32
    )
    probe_number = jnp.arange(probe_count, dtype=jnp.int32)
    earlier = (probe_number[:, None] > probe_number[None, :]).astype(jnp.float32)
    before = right_product(earlier, shard_hot)
    slot_value = jnp.sum(before * shard_hot, axis=1)
    slot_hot = (slot_value[:, None] == jnp.arange(capacity, dtype=jnp.float32)[None, :]).astype(
        jnp.float32
    )
    dispatch = (shard_hot[:, :, None] * slot_hot[:, None, :]).reshape(probe_count, slot_total)
    query_dispatch = jnp.sum(dispatch.reshape(per_dev, probes, slot_total), axis=1)
    send_rows = left_product(query_dispatch, queries).reshape(shards, capacity, emb_width)
    id_values = left_product(dispatch, (within + 1).astype(jnp.float32)[:, None])
    send_ids = (id_values[:, 0] - 1.0).astype(jnp.int32).reshape(shards, capacity)
    got_rows, got_ids = (
        lax.all_to_all(send_rows, "lists", split_axis=0, concat_axis=0, tiled=True),
        lax.all_to_all(send_ids, "lists", split_axis=0, concat_axis=0, tiled=True),
    )
    blocking = 512
    block_count = slot_total // blocking
    row_blocks = got_rows.reshape(block_count, blocking, emb_width)
    id_blocks = got_ids.reshape(block_count, blocking)
    list_ends = jnp.cumsum(list_sizes[0])
    position = jnp.arange(passages.shape[0], dtype=jnp.int32)
    owner_list = jnp.sum((position[:, None] >= list_ends[None, :]).astype(jnp.int32), axis=1)

    def weights_of(block_rows, block_ids):
        scores = score_scale * jnp.dot(
            block_rows,
            passages.T,
            precision=lax.Precision.HIGHEST,
            preferred_element_type=jnp.float32,
        )
        member = owner_list[None, :] == block_ids[:, None]
        usable = block_ids >= 0
        row_top = jnp.max(jnp.where(member, scores, -jnp.inf), axis=1)
        row_top = jnp.where(usable, row_top, 0.0)
        expo_terms = jnp.where(member, jnp.exp(scores - row_top[:, None]), 0.0)
        row_norm = jnp.where(usable, jnp.sum(expo_terms, axis=1), 1.0)
        return (expo_terms, row_top, row_norm)

    def forward_plain(inputs):
        expo_terms, row_top, row_norm = weights_of(inputs[0], inputs[1])
        return (row_top, row_norm)

    row_top, row_norm = lax.map(forward_plain, (row_blocks, id_blocks))
    back_top, back_norm = (
        lax.all_to_all(
            row_top.reshape(shards, capacity), "lists", split_axis=0, concat_axis=0, tiled=True
        ),
        lax.all_to_all(
            row_norm.reshape(shards, capacity), "lists", split_axis=0, concat_axis=0, tiled=True
        ),
    )
    back_stats = jnp.stack([back_top.reshape(-1), back_norm.reshape(-1)], axis=1)
    probe_stats = right_product(dispatch, back_stats)
    probe_top = probe_stats[:, 0].reshape(per_dev, probes)
    probe_norm = probe_stats[:, 1].reshape(per_dev, probes)
    query_peak = jnp.max(probe_top, axis=1)
    probe_mass = probe_norm * jnp.exp(probe_top - query_peak[:, None])
    mass_total = jnp.sum(probe_mass, axis=1)
    probe_share = probe_mass / mass_total[:, None]
    log_share = (
        jnp.log(probe_norm) + (probe_top - query_peak[:, None]) - jnp.log(mass_total)[:, None]
    )
    log_target = jax.nn.log_softmax(reader_logits, axis=1)
    reader_share = jnp.exp(log_target)
    query_loss = jnp.sum(reader_share * (log_target - log_share), axis=1)
    coefficient = (probe_share - reader_share) / probe_norm
    send_coeff = left_product(dispatch, coefficient.reshape(-1, 1))[:, 0].reshape(shards, capacity)
    got_coeff = lax.all_to_all(send_coeff, "lists", split_axis=0, concat_axis=0, tiled=True)
    coeff_blocks = got_coeff.reshape(block_count, blocking)
    start_acc = jnp.zeros((passages.shape[0], emb_width), jnp.float32)

    def passage_term(block_rows, block_ids, block_coeff):
        expo_terms, unused_top, unused_norm = weights_of(block_rows, block_ids)
        weight = expo_terms * block_coeff[:, None]
        term = score_scale * lax.dot_general(
            weight,
            block_rows,
            (((0,), (0,)), ((), ())),
            precision=lax.Precision.HIGHEST,
            preferred_element_type=jnp.float32,
        )
        return (weight, term)

    def backward_plain(passage_acc, inputs):
        weight, term = passage_term(inputs[0], inputs[1], inputs[2])
        query_part = score_scale * jnp.dot(
            weight, passages, precision=lax.Precision.HIGHEST, preferred_element_type=jnp.float32
        )
        return (passage_acc + term, query_part)

    passage_acc, query_parts = lax.scan(
        backward_plain, start_acc, (row_blocks, id_blocks, coeff_blocks)
    )
    back_parts = lax.all_to_all(
        query_parts.reshape(shards, capacity, emb_width),
        "lists",
        split_axis=0,
        concat_axis=0,
        tiled=True,
    )
    query_grad = right_product(query_dispatch, back_parts.reshape(slot_total, emb_width))
    passage_grad = lax.psum_scatter(passage_acc, "qb", scatter_dimension=0, tiled=True)
    return (query_grad, passage_grad, query_loss)


def solution(mesh):
    return jax.shard_map(
        local,
        mesh=mesh,
        in_specs=(
            P(("lists", "qb"), None),
            P(("lists", "qb"), None),
            P(("lists", "qb"), None),
            P(("lists", "qb"), None),
            P("lists", None),
            P("lists", None),
        ),
        out_specs=(P(("lists", "qb"), None), P(("lists", "qb"), None), P(("lists", "qb"))),
        check_vma=False,
    )
```

profile of v0, /device:TPU:2, one launch (start us, length us, event | category | flops | bytes accessed | tf_op | source)
XLA Modules:
  0.0 230.7 jit_solution(17323934524730721825)
XLA Ops:
  9.3 7.4 %fusion.32 = f32[1,64,16]{2,0,1:T(1,128)S(1)} fusion(f32[512,1,1]{0,1,2:T(1,128)S(1)} %reshape.186, f32[512,16]{0,1:T(8,128)S(1)} %fusion.46, f32[512,64]{0,1:T(8,128)S(1)} %fusion.44), kind=kOutput, calls=%fused_computation.45 | convolution fusion | flops 6815744 | bytes 169984 | tf_op jit(solution)/shard_map/dot_general | solution.py:10
  17.3 10.7 %all-to-all-start = ((s32[64,1,16]{2,1,0:T(1,128)}), s32[64,1,16]{2,1,0:T(1,128)S(1)}, u32[]{:S(2)}, u32[]{:S(2)}) async-start(s32[64,1,16]{2,1,0:T(1,128)} %bitcast.11), calls=%async_computation | async-start | bytes 65536 | tf_op jit(solution)/shard_map/all_to_all | solution.py:52
  28.3 9.0 %reshape.191 = f32[32,16,1024]{1,0,2:T(8,128)} reshape(f32[512,64,16]{0,2,1:T(8,128)S(1)} %broadcast_multiply_fusion) | data formatting | bytes 4194304 | tf_op jit(solution)/shard_map/mul | solution.py:45
  37.3 8.2 %reduce_sum.67 = f32[32,1024]{0,1:T(8,128)S(1)} reduce(f32[32,16,1024]{1,0,2:T(8,128)} %reshape.191, f32[]{:T(128)} %constant.42.clone.1), dimensions={1}, to_apply=%region_1.0 | reduce | flops 491520 | bytes 2228228
  47.5 10.3 %all-to-all-start.1 = ((f32[64,16,128]{2,1,0:T(8,128)}), f32[64,16,128]{2,1,0:T(8,128)S(1)}, u32[]{:S(2)}, u32[]{:S(2)}) async-start(f32[64,16,128]{2,1,0:T(8,128)} %fusion.47), calls=%async_computation.1 | async-start | bytes 1048576 | tf_op jit(solution)/shard_map/all_to_all | solution.py:51
  64.6 10.0 %all-to-all-done.1 = f32[64,16,128]{2,1,0:T(8,128)S(1)} async-done(((f32[64,16,128]{2,1,0:T(8,128)}), f32[64,16,128]{2,1,0:T(8,128)S(1)}, u32[]{:S(2)}, u32[]{:S(2)}) %all-to-all-start.1) | async-done | bytes 524320 | tf_op jit(solution)/shard_map/all_to_all | solution.py:51
  74.5 13.3 %while.25 = (s32[]{:T(128)}, f32[2,512]{1,0:T(2,128)}, f32[2,512]{1,0:T(2,128)}, s32[2,512]{1,0:T(2,128)}, s32[768]{0:T(1024)}, /*index=5*/f32[2,512,128]{2,1,0:...) while((s32[]{:T(128)}, f32[2,512]{1,0:T(2,128)}, f32[2,512]{1,0:T(2,128)}, s32[2,512]{1,0:T(2,128)}, ...), condition=%wide.region_7.8_spmd, body=%wide.region_4.7_spmd.sunk | while | flops 607127040 | bytes 3874985 | solution.py:81
  75.2 2.2 fusion.77
  81.9 2.2 fusion.77
  89.2 7.1 %all-to-all-start.2 = ((f32[64,1,16]{2,1,0:T(1,128)}), f32[64,1,16]{2,1,0:T(1,128)}, u32[]{:S(2)}, u32[]{:S(2)}) async-start(f32[64,1,16]{2,1,0:T(1,128)} %bitcast.102), calls=%async_computation.2 | async-start | bytes 65536 | tf_op jit(solution)/shard_map/all_to_all | solution.py:83
  100.3 4.5 %all-to-all-done.2 = f32[64,1,16]{2,1,0:T(1,128)} async-done(((f32[64,1,16]{2,1,0:T(1,128)}), f32[64,1,16]{2,1,0:T(1,128)}, u32[]{:S(2)}, u32[]{:S(2)}) %all-to-all-start.2) | async-done | bytes 4128 | tf_op jit(solution)/shard_map/all_to_all | solution.py:83
  104.9 6.0 %all-to-all-start.3 = ((f32[64,1,16]{2,1,0:T(1,128)}), f32[64,1,16]{2,1,0:T(1,128)}, u32[]{:S(2)}, u32[]{:S(2)}) async-start(f32[64,1,16]{2,1,0:T(1,128)} %bitcast.101), calls=%async_computation.3 | async-start | bytes 65536 | tf_op jit(solution)/shard_map/all_to_all | solution.py:86
  116.5 2.7 %all-to-all-done.3 = f32[64,1,16]{2,1,0:T(1,128)} async-done(((f32[64,1,16]{2,1,0:T(1,128)}), f32[64,1,16]{2,1,0:T(1,128)}, u32[]{:S(2)}, u32[]{:S(2)}) %all-to-all-start.3) | async-done | bytes 4128 | tf_op jit(solution)/shard_map/all_to_all | solution.py:86
  126.7 8.9 %fusion.37 = f32[64,1,16]{2,1,0:T(1,128)} fusion(f32[512,1,1]{0,1,2:T(1,128)S(1)} %reshape.189, f32[512,16]{0,1:T(8,128)} %copy-done.7, f32[512,64]{0,1:T(8,128)} %copy-done.4), kind=kOutput, calls=%fused_computation.51 | convolution fusion | flops 6815744 | bytes 169984 | tf_op jit(solution)/shard_map/dot_general | solution.py:10
  135.7 7.6 %all-to-all-start.4 = ((f32[64,1,16]{2,1,0:T(1,128)}), f32[64,1,16]{2,1,0:T(1,128)S(1)}, u32[]{:S(2)}, u32[]{:S(2)}) async-start(f32[64,1,16]{2,1,0:T(1,128)} %fusion.37), calls=%async_computation.4 | async-start | bytes 65536 | tf_op jit(solution)/shard_map/all_to_all | solution.py:106
  143.3 8.5 %all-to-all-done.4 = f32[64,1,16]{2,1,0:T(1,128)S(1)} async-done(((f32[64,1,16]{2,1,0:T(1,128)}), f32[64,1,16]{2,1,0:T(1,128)S(1)}, u32[]{:S(2)}, u32[]{:S(2)}) %all-to-all-start.4) | async-done | bytes 4128 | tf_op jit(solution)/shard_map/all_to_all | solution.py:106
  152.7 16.6 %while.26 = (s32[]{:T(128)}, f32[768,128]{1,0:T(8,128)S(1)}, f32[2,512,128]{2,1,0:T(8,128)}, s32[768]{0:T(1024)}, s32[2,512]{1,0:T(2,128)}, /*index=5*/f32[2,512...) while((s32[]{:T(128)}, f32[768,128]{1,0:T(8,128)S(1)}, ...), condition=%wide.region_14.15_spmd.clone, body=%wide.region_12.14_spmd.clone.sunk | while | flops 1817018880 | bytes 7131803 | solution.py:129
  155.7 2.3 %fusion.86 = f32[2,512,128]{2,1,0:T(8,128)} fusion(f32[2,512,128]{2,1,0:T(8,128)} %get-tuple-element.298, s32[]{:T(128)} %get-tuple-element.296, f32[768,128]{1,0:T(8,128)S(1)} %get-tuple-element.312, f32[512,768]{1,0:T(8,128)S(1)} %get-tuple-element.257, f32[512]{0:T(512)S(1)} %bitcast.103, f32[512]{0:T(512)S(1)} %compare_select_fusion.13, ...), kind=kOutput, calls=%fused_computation.21.clone.1 | convolution fusion | flops 605618176 | bytes 2237952 | tf_op jit(solution)/shard_map/while/body/eval_jaxpr/dot_general | solution.py:124
  158.0 3.0 %fusion.85 = f32[768,128]{1,0:T(8,128)S(1)} fusion(f32[512,768]{1,0:T(8,128)S(1)} %get-tuple-element.257, f32[512]{0:T(512)S(1)} %bitcast.104, f32[512]{0:T(512)S(1)} %compare_select_fusion.13, s32[768]{0:T(1024)S(1)} %copy-done.3, s32[512]{0:T(512)S(1)} %bitcast.98, f32[768,128]{1,0:T(8,128)S(1)} %get-tuple-element.297, ...), kind=kOutput, calls=%fused_computation.18.clone.1 | convolution fusion | flops 605847552 | bytes 2631685 | tf_op jit(solution)/shard_map/while/body/eval_jaxpr/dot_general | solution.py:113
  164.0 2.3 %fusion.86 = f32[2,512,128]{2,1,0:T(8,128)} fusion(f32[2,512,128]{2,1,0:T(8,128)} %get-tuple-element.298, s32[]{:T(128)} %get-tuple-element.296, f32[768,128]{1,0:T(8,128)S(1)} %get-tuple-element.312, f32[512,768]{1,0:T(8,128)S(1)} %get-tuple-element.257, f32[512]{0:T(512)S(1)} %bitcast.103, f32[512]{0:T(512)S(1)} %compare_select_fusion.13, ...), kind=kOutput, calls=%fused_computation.21.clone.1 | convolution fusion | flops 605618176 | bytes 2237952 | tf_op jit(solution)/shard_map/while/body/eval_jaxpr/dot_general | solution.py:124
  166.3 3.0 %fusion.85 = f32[768,128]{1,0:T(8,128)S(1)} fusion(f32[512,768]{1,0:T(8,128)S(1)} %get-tuple-element.257, f32[512]{0:T(512)S(1)} %bitcast.104, f32[512]{0:T(512)S(1)} %compare_select_fusion.13, s32[768]{0:T(1024)S(1)} %copy-done.3, s32[512]{0:T(512)S(1)} %bitcast.98, f32[768,128]{1,0:T(8,128)S(1)} %get-tuple-element.297, ...), kind=kOutput, calls=%fused_computation.18.clone.1 | convolution fusion | flops 605847552 | bytes 2631685 | tf_op jit(solution)/shard_map/while/body/eval_jaxpr/dot_general | solution.py:113
  169.3 5.5 %all-to-all-start.5 = ((f32[64,16,128]{2,1,0:T(8,128)}), f32[64,16,128]{2,1,0:T(8,128)S(1)}, u32[]{:S(2)}, u32[]{:S(2)}) async-start(f32[64,16,128]{2,1,0:T(8,128)} %bitcast.23), calls=%async_computation.5 | async-start | bytes 1048576 | tf_op jit(solution)/shard_map/all_to_all | solution.py:132
  175.5 16.0 %all-to-all-done.5 = f32[64,16,128]{2,1,0:T(8,128)S(1)} async-done(((f32[64,16,128]{2,1,0:T(8,128)}), f32[64,16,128]{2,1,0:T(8,128)S(1)}, u32[]{:S(2)}, u32[]{:S(2)}) %all-to-all-start.5) | async-done | bytes 524320 | tf_op jit(solution)/shard_map/all_to_all | solution.py:132
  193.1 30.7 %reduce-scatter.2.cloned.1.call-done = f32[96,128]{1,0:T(8,128)} async-done(((f32[768,128]{1,0:T(8,128)}), f32[96,128]{1,0:T(8,128)}) %reduce-scatter.2.cloned.1.call-update) | async-done | bytes 49168 | tf_op jit(solution)/shard_map/reduce_scatter | solution.py:140
  (90 shorter events, 47.9 us)
Async XLA Ops:
  7.2 38.4 %copy-start = (f32[32,128]{1,0:T(8,128)S(1)}, f32[32,128]{1,0:T(8,128)}, u32[]{:S(2)}) copy-start(f32[32,128]{1,0:T(8,128)} %param.10) | copy-start | bytes 49156
  8.1 20.2 %copy-start.4 = (f32[512,64]{0,1:T(8,128)}, f32[512,64]{0,1:T(8,128)S(1)}, u32[]{:S(2)}) copy-start(f32[512,64]{0,1:T(8,128)S(1)} %fusion.44) | copy-start | bytes 393220
  8.4 19.9 %copy-start.7 = (f32[512,16]{0,1:T(8,128)}, f32[512,16]{0,1:T(8,128)S(1)}, u32[]{:S(2)}) copy-start(f32[512,16]{0,1:T(8,128)S(1)} %fusion.46) | copy-start | bytes 98308
  17.3 29.6 %all-to-all-start = ((s32[64,1,16]{2,1,0:T(1,128)}), s32[64,1,16]{2,1,0:T(1,128)S(1)}, u32[]{:S(2)}, u32[]{:S(2)}) async-start(s32[64,1,16]{2,1,0:T(1,128)} %bitcast.11), calls=%async_computation | async-start | bytes 65536 | tf_op jit(solution)/shard_map/all_to_all | solution.py:52
  45.5 29.0 %copy-start.1 = (f32[768,128]{1,0:T(8,128)S(1)}, f32[768,128]{1,0:T(8,128)}, u32[]{:S(2)}) copy-start(f32[768,128]{1,0:T(8,128)} %param.14) | copy-start | bytes 1179652
  46.9 0.6 copy-start.8
  47.5 27.0 %all-to-all-start.1 = ((f32[64,16,128]{2,1,0:T(8,128)}), f32[64,16,128]{2,1,0:T(8,128)S(1)}, u32[]{:S(2)}, u32[]{:S(2)}) async-start(f32[64,16,128]{2,1,0:T(8,128)} %fusion.47), calls=%async_computation.1 | async-start | bytes 1048576 | tf_op jit(solution)/shard_map/all_to_all | solution.py:51
  74.5 2.9 %copy-start.2 = (s32[768]{0:T(1024)S(1)}, s32[768]{0:T(1024)}, u32[]{:S(2)}) copy-start(s32[768]{0:T(1024)} %get-tuple-element.281) | copy-start | bytes 9220 | tf_op jit(solution)/shard_map/while
  75.2 2.7 %copy-start.6 = (s32[2,512]{1,0:T(2,128)S(1)}, s32[2,512]{1,0:T(2,128)}, u32[]{:S(2)}) copy-start(s32[2,512]{1,0:T(2,128)} %get-tuple-element.280) | copy-start | bytes 12292 | tf_op jit(solution)/shard_map/while
  81.2 2.9 %copy-start.2 = (s32[768]{0:T(1024)S(1)}, s32[768]{0:T(1024)}, u32[]{:S(2)}) copy-start(s32[768]{0:T(1024)} %get-tuple-element.281) | copy-start | bytes 9220 | tf_op jit(solution)/shard_map/while
  81.9 2.7 %copy-start.6 = (s32[2,512]{1,0:T(2,128)S(1)}, s32[2,512]{1,0:T(2,128)}, u32[]{:S(2)}) copy-start(s32[2,512]{1,0:T(2,128)} %get-tuple-element.280) | copy-start | bytes 12292 | tf_op jit(solution)/shard_map/while
  89.2 15.6 %all-to-all-start.2 = ((f32[64,1,16]{2,1,0:T(1,128)}), f32[64,1,16]{2,1,0:T(1,128)}, u32[]{:S(2)}, u32[]{:S(2)}) async-start(f32[64,1,16]{2,1,0:T(1,128)} %bitcast.102), calls=%async_computation.2 | async-start | bytes 65536 | tf_op jit(solution)/shard_map/all_to_all | solution.py:83
  104.9 14.3 %all-to-all-start.3 = ((f32[64,1,16]{2,1,0:T(1,128)}), f32[64,1,16]{2,1,0:T(1,128)}, u32[]{:S(2)}, u32[]{:S(2)}) async-start(f32[64,1,16]{2,1,0:T(1,128)} %bitcast.101), calls=%async_computation.3 | async-start | bytes 65536 | tf_op jit(solution)/shard_map/all_to_all | solution.py:86
  135.7 16.2 %all-to-all-start.4 = ((f32[64,1,16]{2,1,0:T(1,128)}), f32[64,1,16]{2,1,0:T(1,128)S(1)}, u32[]{:S(2)}, u32[]{:S(2)}) async-start(f32[64,1,16]{2,1,0:T(1,128)} %fusion.37), calls=%async_computation.4 | async-start | bytes 65536 | tf_op jit(solution)/shard_map/all_to_all | solution.py:106
  152.7 3.0 %copy-start.3 = (s32[768]{0:T(1024)S(1)}, s32[768]{0:T(1024)}, u32[]{:S(2)}) copy-start(s32[768]{0:T(1024)} %get-tuple-element.309) | copy-start | bytes 9220 | tf_op jit(solution)/shard_map/while
  161.0 3.0 %copy-start.3 = (s32[768]{0:T(1024)S(1)}, s32[768]{0:T(1024)}, u32[]{:S(2)}) copy-start(s32[768]{0:T(1024)} %get-tuple-element.309) | copy-start | bytes 9220 | tf_op jit(solution)/shard_map/while
  169.3 5.6 %copy-start.5 = (f32[768,128]{1,0:T(8,128)}, f32[768,128]{1,0:T(8,128)S(1)}, u32[]{:S(2)}) copy-start(f32[768,128]{1,0:T(8,128)S(1)} %get-tuple-element.87) | copy-start | bytes 1179652
  169.3 22.2 %all-to-all-start.5 = ((f32[64,16,128]{2,1,0:T(8,128)}), f32[64,16,128]{2,1,0:T(8,128)S(1)}, u32[]{:S(2)}, u32[]{:S(2)}) async-start(f32[64,16,128]{2,1,0:T(8,128)} %bitcast.23), calls=%async_computation.5 | async-start | bytes 1048576 | tf_op jit(solution)/shard_map/all_to_all | solution.py:132
  174.8 49.0 %reduce-scatter.2.cloned.1.call-start = ((), (), s32[]{:S(2)}) async-start(), calls=%async_computation.7 | async-start | bytes 442368 | tf_op jit(solution)/shard_map/reduce_scatter | solution.py:140
Sparse Core Ops, SparseCore 0:
  179.0 44.7 reduce-scatter.1
where the time goes:
time: 232 us; the launch traced here: 231 us
  waiting for transfers between devices  73.1 us (32%)
  starting transfers between devices  47.3 us (20%)
  matrix products  41 us (18%)
  local copies, waits for them, and re-layouts  29.1 us (13%)
  other arithmetic  25.7 us (11%)
  between operations  14.3 us (6%)
    reduce_scatter x1, waiting for transfers between devices, local(): lax.psum_scatter(passage_acc, 'qb', scatter_dimension=0, tiled=True)  30.7 us
    dot_general x3, matrix products, left_product(): lax.dot_general(table, values, (((0,), (0,)), ((), ())), precision=lax.Pr...  17.7 us
    all_to_all x1, waiting for transfers between devices, local(): lax.all_to_all(query_parts.reshape(shards, capacity, emb_width), 'lists',...  16 us
    all_to_all x1, starting transfers between devices, local(): lax.all_to_all(send_ids, 'lists', split_axis=0, concat_axis=0, tiled=True)  10.7 us
    all_to_all x1, starting transfers between devices, local(): lax.all_to_all(send_rows, 'lists', split_axis=0, concat_axis=0, tiled=True)  10.3 us
    all_to_all x1, waiting for transfers between devices, local(): lax.all_to_all(send_rows, 'lists', split_axis=0, concat_axis=0, tiled=True)  9.98 us
    mul x1, local copies, waits for them, and re-layouts, local(): shard_hot[:, :, None] * slot_hot[:, None, :]  9.02 us
    dot_general x4, matrix products, weights_of(): jnp.dot(block_rows, passages.T, precision=lax.Precision.HIGHEST, preferre...  8.97 us
  transfers between devices with their start and end apart: 7, of which 6 were waited for; matrix products, arithmetic and copies ran while one was open for 15% of the time, Pallas kernels for 0%

commit v1 on v0

v1 whole, which is shorter than its diff:
```python
import functools
import math

import jax
import jax.numpy as jnp
from jax import lax
from jax.experimental import pallas as pl
from jax.experimental.pallas import tpu as pltpu
from jax.sharding import PartitionSpec as P

MESH = pl.DeviceIdType.MESH
F32, BF16, I32 = jnp.float32, jnp.bfloat16, jnp.int32
LOW = -1e30
GROUP = 8


def split3(x):
    hi = x.astype(BF16)
    rest = x - hi.astype(F32)
    mid = rest.astype(BF16)
    low = (rest - mid.astype(F32)).astype(BF16)
    return hi, mid, low


def split2(x):
    hi = x.astype(BF16)
    return hi, (x - hi.astype(F32)).astype(BF16)


def mm(a, b):
    return jnp.dot(a, b, preferred_element_type=F32)


def mm_nt(a, b):
    return lax.dot_general(a, b, (((1,), (1,)), ((), ())), preferred_element_type=F32)


def mm_tn(a, b):
    return lax.dot_general(a, b, (((0,), (0,)), ((), ())), preferred_element_type=F32)


def kernel(
    shards,
    groups,
    cap,
    q_hbm,
    lg_hbm,
    ps_hbm,
    pw_hbm,
    p_hbm,
    ls_hbm,
    qg_ref,
    pg_ref,
    loss_ref,
    q_v,
    lg_v,
    ps_v,
    pw_v,
    p_v,
    ls_v,
    meta_s,
    meta_r,
    rows_s,
    rows_r,
    stat_s,
    stat_r,
    coef_s,
    coef_r,
    u_s,
    u_r,
    z_s,
    z_r,
    expand,
    disp,
    logt,
    acoef,
    pcat,
    ptr,
    owner,
    eh,
    el,
    rch,
    rcm,
    in_sem,
    meta_ss,
    meta_rs,
    rows_ss,
    rows_rs,
    stat_ss,
    stat_rs,
    coef_ss,
    coef_rs,
    u_ss,
    u_rs,
    z_ss,
    z_rs,
):
    per_dev, emb = q_v.shape
    probes = ps_v.shape[1]
    pass_dev = p_v.shape[0]
    part = pass_dev // groups
    chunks = shards // GROUP
    width = GROUP * cap
    slots = shards * cap
    scale = 1.0 / math.sqrt(emb)
    me = lax.axis_index("lists")
    qb = lax.axis_index("qb")

    def peer(j):
        return {"lists": lax.rem(me + j, shards)}

    def source(j):
        return {"lists": lax.rem(me - j + shards, shards)}

    def to(src, dst, ss, rs, device):
        return pltpu.make_async_remote_copy(
            src_ref=src, dst_ref=dst, send_sem=ss, recv_sem=rs, device_id=device, device_id_type=MESH
        )

    order = [
        (groups // 2 + ((i % 2) * 2 - 1) * ((i + 1) // 2)) % groups for i in range(groups)
    ]
    small = [(q_hbm, q_v), (ps_hbm, ps_v), (pw_hbm, pw_v), (lg_hbm, lg_v), (ls_hbm, ls_v)]
    loads = [pltpu.make_async_copy(a, b, in_sem.at[i]) for i, (a, b) in enumerate(small)]
    for i, d in enumerate(order):
        start = pl.multiple_of(lax.rem(qb + d, groups) * part, part)
        loads.append(
            pltpu.make_async_copy(
                p_hbm.at[pl.ds(start, part)], p_v.at[pl.ds(i * part, part)], in_sem.at[len(small) + i]
            )
        )
    for load in loads:
        load.start()

    barrier = pltpu.get_barrier_semaphore()

    def greet(j, carry):
        pl.semaphore_signal(barrier, inc=1, device_id=peer(j), device_id_type=MESH)
        return carry

    lax.fori_loop(1, shards, greet, 0)
    for d in range(1, groups):
        pl.semaphore_signal(
            barrier, inc=1, device_id={"qb": lax.rem(qb + d, groups)}, device_id_type=MESH
        )

    expand[...] = (
        lax.broadcasted_iota(I32, (shards, slots), 1) // cap
        == lax.broadcasted_iota(I32, (shards, slots), 0)
    ).astype(BF16)
    place = (lax.rem(lax.broadcasted_iota(I32, (per_dev, slots), 1), cap) + 1).astype(F32)
    tri = (
        lax.broadcasted_iota(I32, (per_dev, per_dev), 1)
        <= lax.broadcasted_iota(I32, (per_dev, per_dev), 0)
    ).astype(BF16)
    shard_lane = lax.broadcasted_iota(I32, (per_dev, shards), 1)
    for load in loads[:3]:
        load.wait()
    ps = ps_v[...]
    rel = jnp.where(ps >= me, ps - me, ps - me + shards)
    within = pw_v[...]
    w1 = jnp.zeros((per_dev, shards), F32)
    for k in range(probes):
        w1 = jnp.where(rel[:, k : k + 1] == shard_lane, (within[:, k : k + 1] + 1).astype(F32), w1)
    hot = w1 > 0.0
    rank = mm(tri, hot.astype(BF16))
    slot1 = jnp.where(hot, rank, 0.0)
    both = mm(jnp.concatenate([slot1, w1], axis=0).astype(BF16), expand[...])
    mask = both[:per_dev] == place
    disp[...] = mask.astype(F32)
    ids = jnp.sum(jnp.where(mask, both[per_dev:], 0.0), axis=0, keepdims=True)
    for c in range(chunks):
        meta_s[c] = ids[:, c * width : (c + 1) * width]
    q_scaled = q_v[...] * scale
    q3 = jnp.concatenate(split3(q_scaled), axis=0)
    for c in range(chunks):
        d1 = disp[:, c * width : (c + 1) * width].astype(BF16)
        block = mm_tn(jnp.concatenate([d1, d1, d1], axis=0), q3)
        rows_s[pl.ds(c * GROUP, GROUP)] = block.reshape(GROUP, cap, emb)

    pl.semaphore_wait(barrier, shards - 1 + groups - 1)

    def send_meta(j, carry):
        c = j // GROUP
        to(meta_s.at[c], meta_r.at[j], meta_ss, meta_rs.at[c], peer(j)).start()
        return carry

    def send_rows(j, carry):
        c = j // GROUP
        to(rows_s.at[j], rows_r.at[j], rows_ss, rows_rs.at[c], peer(j)).start()
        return carry

    def send_both(j, carry):
        return send_rows(j, send_meta(j, carry))

    lax.fori_loop(1, shards, send_both, 0)
    meta_r[0] = meta_s[0]
    rows_r[0] = rows_s[0]

    for load in loads[3:]:
        load.wait()
    p = p_v[...]
    ph, pm, plow = split3(p)
    pcat[...] = jnp.concatenate([ph, pm, ph, plow, ph, pm], axis=1)
    pth, ptm = split2(p.T)
    ptr[:, :pass_dev] = pth
    ptr[:, pass_dev:] = ptm
    end = jnp.zeros((1, 1), I32)
    for i, d in enumerate(order):
        first = lax.rem(qb + d, groups) * part
        number = lax.broadcasted_iota(I32, (part, width), 0) + first
        end = jnp.zeros((1, 1), I32)
        own = jnp.ones((part, width), F32)
        for g in range(ls_v.shape[1]):
            end = end + ls_v[:, g : g + 1]
            own = own + jnp.where(number >= end, 1.0, 0.0)
        owner[i * part : (i + 1) * part, :] = own

    lg = lg_v[...]
    lg = lg - jnp.max(lg, axis=1, keepdims=True)
    lt = lg - jnp.log(jnp.sum(jnp.exp(lg), axis=1, keepdims=True))
    lt_shard = jnp.zeros((per_dev, shards), F32)
    for k in range(probes):
        lt_shard = jnp.where(rel[:, k : k + 1] == shard_lane, lt[:, k : k + 1], lt_shard)
    lt3 = mm(jnp.concatenate(split3(lt_shard), axis=0), expand[...])
    logt[...] = lt3[:per_dev] + lt3[per_dev : 2 * per_dev] + lt3[2 * per_dev :]

    lane = lax.broadcasted_iota(I32, (1, width), 1) // cap

    def gather_row(ref, c, row):
        out = jnp.zeros((1, width), F32)
        for jj in range(GROUP):
            out = jnp.where(lane == jj, ref[c * GROUP + jj, row : row + 1, :], out)
        return out

    def wait_chunk(ref, sems, c):
        @pl.when(c == 0)
        def _():
            view = ref.at[pl.ds(1, GROUP - 1)]
            to(view, view, rows_ss, sems.at[0], peer(1)).wait_recv()

        @pl.when(c > 0)
        def _():
            view = ref.at[pl.ds(c * GROUP, GROUP)]
            to(view, view, rows_ss, sems.at[c], peer(1)).wait_recv()

    def forward(c, carry):
        wait_chunk(meta_r, meta_rs, c)
        ident = gather_row(meta_r, c, 0)
        wait_chunk(rows_r, rows_rs, c)
        rows = rows_r[pl.ds(c * GROUP, GROUP)].reshape(width, emb)
        rh, rm, rl = split3(rows)
        score = mm_nt(pcat[...], jnp.concatenate([rh, rh, rm, rh, rl, rm], axis=1))
        score = jnp.where(owner[...] == ident, score, LOW)
        top = jnp.max(score, axis=0, keepdims=True)
        expo = jnp.exp(score - top)
        norm = jnp.sum(expo, axis=0, keepdims=True)
        stat_s[c, 0:1, :] = top
        stat_s[c, 1:2, :] = norm

        def send_stat(jj, carry):
            j = c * GROUP + jj
            to(stat_s.at[c], stat_r.at[j], stat_ss, stat_rs, source(j)).start()
            return carry

        lax.fori_loop(jnp.where(c == 0, 1, 0), GROUP, send_stat, 0)
        hi, lo = split2(expo)
        at = pl.ds(pl.multiple_of(c * width, width), width)
        eh[:, at] = hi
        el[:, at] = lo
        return carry

    lax.fori_loop(0, chunks, forward, 0)
    stat_r[0] = stat_s[0]

    def query_part(c, carry):
        at = pl.ds(pl.multiple_of(c * width, width), width)
        hi, lo = eh[:, at], el[:, at]
        part_t = mm(ptr[:, :pass_dev], hi) + mm(ptr[:, :pass_dev], lo) + mm(ptr[:, pass_dev:], hi)
        u_s[pl.ds(c * GROUP, GROUP)] = part_t.T.reshape(GROUP, cap, emb)
        return carry

    lax.fori_loop(0, chunks, query_part, 0)
    u_r[0] = u_s[0]

    rest = stat_r.at[pl.ds(1, shards - 1)]
    to(rest, rest, stat_ss, stat_rs, peer(1)).wait_recv()
    top = jnp.concatenate([gather_row(stat_r, c, 0) for c in range(chunks)], axis=1)
    norm = jnp.concatenate([gather_row(stat_r, c, 1) for c in range(chunks)], axis=1)
    mask = disp[...] > 0.0
    peak = jnp.max(jnp.where(mask, top, LOW), axis=1, keepdims=True)
    gap = jnp.where(mask, top - peak, 0.0)
    mass = jnp.where(mask, norm * jnp.exp(gap), 0.0)
    total = jnp.sum(mass, axis=1, keepdims=True)
    share = mass / total
    log_target = logt[...]
    target = jnp.exp(log_target)
    coef = jnp.where(mask, (share - target) / norm, 0.0)
    coef_row = jnp.sum(coef, axis=0, keepdims=True)
    for c in range(chunks):
        coef_s[c] = coef_row[:, c * width : (c + 1) * width]

    def send_coef(j, carry):
        to(coef_s.at[j // GROUP], coef_r.at[j], coef_ss, coef_rs, peer(j)).start()
        return carry

    lax.fori_loop(1, shards, send_coef, 0)
    coef_r[0] = coef_s[0]

    def send_u(j, carry):
        to(u_s.at[j], u_r.at[j], u_ss, u_rs, source(j)).start()
        return carry

    lax.fori_loop(1, shards, send_u, 0)
    acoef[...] = coef * scale
    log_share = jnp.log(norm) + gap - jnp.log(total)
    term = jnp.where(mask, target * (log_target - log_share), 0.0)
    loss_ref[...] = jnp.sum(term, axis=1, keepdims=True)

    rest = coef_r.at[pl.ds(1, shards - 1)]
    to(rest, rest, coef_ss, coef_rs, peer(1)).wait_recv()
    for c in range(chunks):
        column = jnp.broadcast_to(gather_row(coef_r, c, 0), (width, width)).T
        rows = rows_r[c * GROUP : (c + 1) * GROUP].reshape(width, emb)
        hi, mid = split2(rows * column)
        rch[c * width : (c + 1) * width, :] = hi
        rcm[c * width : (c + 1) * width, :] = mid
    per = max(1, groups // 2)
    for h in range(0, groups, per):
        rows_at = slice(h * part, (h + per) * part)
        block = mm(eh[rows_at, :], rch[...]) + mm(el[rows_at, :], rch[...]) + mm(eh[rows_at, :], rcm[...])
        for i in range(h, h + per):
            d = order[i]
            z_s[d] = block[(i - h) * part : (i - h + 1) * part]
            if d != 0:
                to(
                    z_s.at[d], z_r.at[d], z_ss, z_rs, {"qb": lax.rem(qb + d, groups)}
                ).start()

    rest = u_r.at[pl.ds(1, shards - 1)]
    to(rest, rest, u_ss, u_rs, peer(1)).wait_recv()
    qg = jnp.zeros((per_dev, emb), F32)
    for c in range(chunks):
        ah, am = split2(acoef[:, c * width : (c + 1) * width])
        uh, um = split2(u_r[c * GROUP : (c + 1) * GROUP].reshape(width, emb))
        qg = qg + mm(ah, uh) + mm(am, uh) + mm(ah, um)
    qg_ref[...] = qg

    rest = z_r.at[pl.ds(1, groups - 1)]
    to(rest, rest, z_ss, z_rs, {"qb": lax.rem(qb + 1, groups)}).wait_recv()
    out = z_s[0]
    for d in range(1, groups):
        out = out + z_r[d]
    pg_ref[...] = out

    for ref, sem in (
        (meta_r, meta_ss),
        (rows_r, rows_ss),
        (stat_r, stat_ss),
        (coef_r, coef_ss),
        (u_r, u_ss),
    ):
        rest = ref.at[pl.ds(1, shards - 1)]
        to(rest, rest, sem, coef_rs, peer(1)).wait_send()
    rest = z_r.at[pl.ds(1, groups - 1)]
    to(rest, rest, z_ss, z_rs, {"qb": lax.rem(qb + 1, groups)}).wait_send()


def local(shards, groups, queries, reader_logits, probe_shards, probe_within, passages, list_sizes):
    per_dev, emb = queries.shape
    probes = probe_shards.shape[1]
    pass_dev = passages.shape[0]
    cap = min(per_dev, 16)
    chunks = shards // GROUP
    width = GROUP * cap
    slots = shards * cap
    part = pass_dev // groups
    vmem = pltpu.VMEM
    dma = pltpu.SemaphoreType.DMA
    any_spec = pl.BlockSpec(memory_space=pl.ANY)
    vmem_spec = pl.BlockSpec(memory_space=pltpu.VMEM)
    qg, pg, loss = pl.pallas_call(
        functools.partial(kernel, shards, groups, cap),
        out_shape=(
            jax.ShapeDtypeStruct((per_dev, emb), F32),
            jax.ShapeDtypeStruct((part, emb), F32),
            jax.ShapeDtypeStruct((per_dev, 1), F32),
        ),
        in_specs=[any_spec] * 6,
        out_specs=(vmem_spec,) * 3,
        scratch_shapes=[
            vmem((per_dev, emb), F32),
            vmem((per_dev, probes), F32),
            vmem((per_dev, probes), I32),
            vmem((per_dev, probes), I32),
            vmem((pass_dev, emb), F32),
            vmem(list_sizes.shape, I32),
            vmem((chunks, 1, width), F32),
            vmem((shards, 1, width), F32),
            vmem((shards, cap, emb), F32),
            vmem((shards, cap, emb), F32),
            vmem((chunks, 2, width), F32),
            vmem((shards, 2, width), F32),
            vmem((chunks, 1, width), F32),
            vmem((shards, 1, width), F32),
            vmem((shards, cap, emb), F32),
            vmem((shards, cap, emb), F32),
            vmem((groups, part, emb), F32),
            vmem((groups, part, emb), F32),
            vmem((shards, slots), BF16),
            vmem((per_dev, slots), F32),
            vmem((per_dev, slots), F32),
            vmem((per_dev, slots), F32),
            vmem((pass_dev, 6 * emb), BF16),
            vmem((emb, 2 * pass_dev), BF16),
            vmem((pass_dev, width), F32),
            vmem((pass_dev, slots), BF16),
            vmem((pass_dev, slots), BF16),
            vmem((slots, emb), BF16),
            vmem((slots, emb), BF16),
            dma((5 + groups,)),
            dma,
            dma((chunks,)),
            dma,
            dma((chunks,)),
            dma,
            dma,
            dma,
            dma,
            dma,
            dma,
            dma,
            dma,
        ],
        compiler_params=pltpu.CompilerParams(
            collective_id=0, has_side_effects=True, vmem_limit_bytes=40 * 1024 * 1024
        ),
    )(queries, reader_logits, probe_shards, probe_within, passages, list_sizes)
    return qg, pg, loss[:, 0]


def solution(mesh):
    return jax.shard_map(
        functools.partial(local, mesh.shape["lists"], mesh.shape["qb"]),
        mesh=mesh,
        in_specs=(
            P(("lists", "qb"), None),
            P(("lists", "qb"), None),
            P(("lists", "qb"), None),
            P(("lists", "qb"), None),
            P("lists", None),
            P("lists", None),
        ),
        out_specs=(P(("lists", "qb"), None), P(("lists", "qb"), None), P(("lists", "qb"))),
        check_vma=False,
    )
```

time: 232 us -> 63.7 us (0.27)
  the two profiles are of different devices: /device:TPU:2 before, /device:TPU:1 now
where the time goes in v1:
time: 63.7 us; the launch traced here: 63.4 us
  Pallas kernels  57.7 us (91%)
  local copies, waits for them, and re-layouts  4.42 us (7%)
  between operations  0.65 us (1%)
    pallas_call x1, Pallas kernels, local(): pl.pallas_call(functools.partial(kernel, shards, groups, cap), out_shape=...  57.7 us
    unnamed x15, local copies, waits for them, and re-layouts  4.42 us

profile of v1, /device:TPU:1, one launch (start us, length us, event | category | flops | bytes accessed | tf_op | source)
XLA Modules:
  0.0 63.4 jit_solution(7077066236540840675)
XLA Ops:
  0.6 0.0 copy-start.3
  0.6 0.8 %copy.12.lg_hbm = f32[32,16]{1,0:T(8,128)S(1)} copy(f32[32,16]{0,1:T(8,128)} %param.7) | data formatting | bytes 4096 | tf_op args[1]
  1.4 0.0 copy-done.3
  1.4 0.0 copy-start.4
  1.4 0.1 copy.13.ps_hbm
  1.5 0.6 copy-done.4
  2.1 0.0 copy-start.1
  2.1 0.0 copy-start.2
  2.1 0.1 copy.14.pw_hbm
  2.2 0.6 %copy-done.1 = f32[32,128]{1,0:T(8,128)S(1)} copy-done((f32[32,128]{1,0:T(8,128)S(1)}, f32[32,128]{1,0:T(8,128)}, u32[]{:S(2)}) %copy-start.1) | copy-done | bytes 16408
  2.8 0.0 copy-done.2
  2.8 0.0 copy-start
  2.8 1.0 %copy-done = f32[768,128]{1,0:T(8,128)S(1)} copy-done((f32[768,128]{1,0:T(8,128)S(1)}, f32[768,128]{1,0:T(8,128)}, u32[]{:S(2)}) %copy-start) | copy-done | bytes 393240
  3.8 57.7 %shard_map.85 = (f32[32,128]{1,0:T(8,128)S(1)}, f32[96,128]{1,0:T(8,128)S(1)}, f32[32,1]{1,0:T(8,128)S(1)}) custom-call(f32[32,128]{1,0:T(8,128)S(1)} %copy-done.1, f32[32,16]{1,0:T(8,128)S(1)} %copy.12.lg_hbm, s32[32,16]{1,0:T(8,128)S(1)} %copy.13.ps_hbm, s32[32,16]{1,0:T(8,128)S(1)} %copy.14.pw_hbm, f32[768,128]{1,0:T(8,128)S(1)} %copy-done, ...), custom_call_target="tpu_custom_call" | custom-call | tf_op jit(solution)/shard_map/pallas_call | solution.py:382
  61.6 0.6 reduce
  62.2 0.6 copy.17
  62.8 0.6 copy.18
Async XLA Ops:
  0.6 0.8 %copy-start.3 = (s32[32,16]{0,1:T(8,128)S(1)}, s32[32,16]{0,1:T(8,128)}, u32[]{:S(2)}) copy-start(s32[32,16]{0,1:T(8,128)} %param.8) | copy-start | bytes 6148
  1.4 0.7 %copy-start.4 = (s32[32,16]{0,1:T(8,128)S(1)}, s32[32,16]{0,1:T(8,128)}, u32[]{:S(2)}) copy-start(s32[32,16]{0,1:T(8,128)} %param.9) | copy-start | bytes 6148
  2.1 0.7 %copy-start.1 = (f32[32,128]{1,0:T(8,128)S(1)}, f32[32,128]{1,0:T(8,128)}, u32[]{:S(2)}) copy-start(f32[32,128]{1,0:T(8,128)} %q_hbm.1) | copy-start | bytes 49156
  2.1 0.7 %copy-start.2 = (s32[1,8]{1,0:T(1,128)S(1)}, s32[1,8]{1,0:T(1,128)}, u32[]{:S(2)}) copy-start(s32[1,8]{1,0:T(1,128)} %ls_hbm.1) | copy-start | bytes 100
  2.8 1.0 %copy-start = (f32[768,128]{1,0:T(8,128)S(1)}, f32[768,128]{1,0:T(8,128)}, u32[]{:S(2)}) copy-start(f32[768,128]{1,0:T(8,128)} %p_hbm.1) | copy-start | bytes 1179652

commit v2 on v1

--- a/solution.py
+++ b/solution.py
@@ -96,7 +96,7 @@
     z_rs,
 ):
     per_dev, emb = q_v.shape
-    probes = ps_v.shape[1]
+    probes = ps_v.shape[0]
     pass_dev = p_v.shape[0]
     part = pass_dev // groups
     chunks = shards // GROUP
@@ -117,9 +117,7 @@
             src_ref=src, dst_ref=dst, send_sem=ss, recv_sem=rs, device_id=device, device_id_type=MESH
         )
 
-    order = [
-        (groups // 2 + ((i % 2) * 2 - 1) * ((i + 1) // 2)) % groups for i in range(groups)
-    ]
+    order = [3, 5, 4, 2, 6, 1, 7, 0]
     small = [(q_hbm, q_v), (ps_hbm, ps_v), (pw_hbm, pw_v), (lg_hbm, lg_v), (ls_hbm, ls_v)]
     loads = [pltpu.make_async_copy(a, b, in_sem.at[i]) for i, (a, b) in enumerate(small)]
     for i, d in enumerate(order):
@@ -157,11 +155,12 @@
     for load in loads[:3]:
         load.wait()
     ps = ps_v[...]
-    rel = jnp.where(ps >= me, ps - me, ps - me + shards)
-    within = pw_v[...]
-    w1 = jnp.zeros((per_dev, shards), F32)
+    rel = jnp.where(ps >= me, ps - me, ps - me + shards).T
+    within = pw_v[...].T + 1
+    w1 = jnp.zeros((per_dev, shards), I32)
     for k in range(probes):
-        w1 = jnp.where(rel[:, k : k + 1] == shard_lane, (within[:, k : k + 1] + 1).astype(F32), w1)
+        w1 = jnp.where(rel[:, k : k + 1] == shard_lane, within[:, k : k + 1], w1)
+    w1 = w1.astype(F32)
     hot = w1 > 0.0
     rank = mm(tri, hot.astype(BF16))
     slot1 = jnp.where(hot, rank, 0.0)
@@ -217,8 +216,8 @@
         owner[i * part : (i + 1) * part, :] = own
 
     lg = lg_v[...]
-    lg = lg - jnp.max(lg, axis=1, keepdims=True)
-    lt = lg - jnp.log(jnp.sum(jnp.exp(lg), axis=1, keepdims=True))
+    lg = lg - jnp.max(lg, axis=0, keepdims=True)
+    lt = (lg - jnp.log(jnp.sum(jnp.exp(lg), axis=0, keepdims=True))).T
     lt_shard = jnp.zeros((per_dev, shards), F32)
     for k in range(probes):
         lt_shard = jnp.where(rel[:, k : k + 1] == shard_lane, lt[:, k : k + 1], lt_shard)
@@ -315,7 +314,12 @@
     acoef[...] = coef * scale
     log_share = jnp.log(norm) + gap - jnp.log(total)
     term = jnp.where(mask, target * (log_target - log_share), 0.0)
-    loss_ref[...] = jnp.sum(term, axis=1, keepdims=True)
+    diagonal = lax.broadcasted_iota(I32, (per_dev, per_dev), 0) == lax.broadcasted_iota(
+        I32, (per_dev, per_dev), 1
+    )
+    loss_ref[...] = jnp.sum(
+        jnp.where(diagonal, jnp.sum(term, axis=1, keepdims=True), 0.0), axis=0, keepdims=True
+    )
 
     rest = coef_r.at[pl.ds(1, shards - 1)]
     to(rest, rest, coef_ss, coef_rs, peer(1)).wait_recv()
@@ -325,17 +329,48 @@
         hi, mid = split2(rows * column)
         rch[c * width : (c + 1) * width, :] = hi
         rcm[c * width : (c + 1) * width, :] = mid
-    per = max(1, groups // 2)
-    for h in range(0, groups, per):
-        rows_at = slice(h * part, (h + per) * part)
-        block = mm(eh[rows_at, :], rch[...]) + mm(el[rows_at, :], rch[...]) + mm(eh[rows_at, :], rcm[...])
-        for i in range(h, h + per):
-            d = order[i]
-            z_s[d] = block[(i - h) * part : (i - h + 1) * part]
-            if d != 0:
-                to(
-                    z_s.at[d], z_r.at[d], z_ss, z_rs, {"qb": lax.rem(qb + d, groups)}
-                ).start()
+    rc = jnp.concatenate([rch[...], rcm[...]], axis=1)
+
+    def passage_part(h):
+        rows_at = slice(h * part, (h + groups // 2) * part)
+        both = mm(eh[rows_at, :], rc) + mm(el[rows_at, :], rc)
+        block = both[:, :emb] + both[:, emb:]
+        for i in range(groups // 2):
+            z_s[order[h + i]] = block[i * part : (i + 1) * part]
+
+    half = part // 2
+    first, second = pl.ds(0, half), pl.ds(half, half)
+
+    def hop(src, slot, rows_at, step):
+        device = {"qb": lax.rem(qb + step + groups, groups)}
+        return to(src, z_r.at[slot].at[rows_at], z_ss.at[slot], z_rs.at[slot], device)
+
+    every = pl.ds(0, part)
+    passage_part(0)
+    relays = [
+        hop(z_s.at[3], 0, every, 1),
+        hop(z_s.at[5], 1, every, -1),
+        hop(z_s.at[4].at[first], 2, first, 2),
+        hop(z_s.at[4].at[second], 3, second, -2),
+    ]
+    for copy in relays:
+        copy.start()
+    passage_part(groups // 2)
+    direct = [hop(z_s.at[1], 4, every, 1), hop(z_s.at[7], 5, every, -1)]
+    for copy in direct:
+        copy.start()
+    relays[0].wait_recv()
+    relays[2].wait_recv()
+    z_s[2] = z_s[2] + z_r[0]
+    z_s[2, 0:half] = z_s[2, 0:half] + z_r[2, 0:half]
+    direct.append(hop(z_s.at[2], 6, every, 2))
+    direct[2].start()
+    relays[1].wait_recv()
+    relays[3].wait_recv()
+    z_s[6] = z_s[6] + z_r[1]
+    z_s[6, half:] = z_s[6, half:] + z_r[3, half:]
+    direct.append(hop(z_s.at[6], 7, every, -2))
+    direct[3].start()
 
     rest = u_r.at[pl.ds(1, shards - 1)]
     to(rest, rest, u_ss, u_rs, peer(1)).wait_recv()
@@ -346,11 +381,10 @@
         qg = qg + mm(ah, uh) + mm(am, uh) + mm(ah, um)
     qg_ref[...] = qg
 
-    rest = z_r.at[pl.ds(1, groups - 1)]
-    to(rest, rest, z_ss, z_rs, {"qb": lax.rem(qb + 1, groups)}).wait_recv()
     out = z_s[0]
-    for d in range(1, groups):
-        out = out + z_r[d]
+    for slot, copy in enumerate(direct):
+        copy.wait_recv()
+        out = out + z_r[4 + slot]
     pg_ref[...] = out
 
     for ref, sem in (
@@ -362,8 +396,17 @@
     ):
         rest = ref.at[pl.ds(1, shards - 1)]
         to(rest, rest, sem, coef_rs, peer(1)).wait_send()
-    rest = z_r.at[pl.ds(1, groups - 1)]
-    to(rest, rest, z_ss, z_rs, {"qb": lax.rem(qb + 1, groups)}).wait_send()
+    for copy in relays + direct:
+        copy.wait_send()
+
+
+def store(qg_ref, pg_ref, loss_ref, qg_out, pg_out, loss_out, sems):
+    pairs = ((pg_ref, pg_out), (qg_ref, qg_out), (loss_ref, loss_out))
+    copies = [pltpu.make_async_copy(a, b, sems.at[i]) for i, (a, b) in enumerate(pairs)]
+    for copy in copies:
+        copy.start()
+    for copy in copies:
+        copy.wait()
 
 
 def local(shards, groups, queries, reader_logits, probe_shards, probe_within, passages, list_sizes):
@@ -377,22 +420,22 @@
     part = pass_dev // groups
     vmem = pltpu.VMEM
     dma = pltpu.SemaphoreType.DMA
-    any_spec = pl.BlockSpec(memory_space=pl.ANY)
+    hbm_spec = pl.BlockSpec(memory_space=pltpu.HBM)
     vmem_spec = pl.BlockSpec(memory_space=pltpu.VMEM)
     qg, pg, loss = pl.pallas_call(
         functools.partial(kernel, shards, groups, cap),
         out_shape=(
             jax.ShapeDtypeStruct((per_dev, emb), F32),
             jax.ShapeDtypeStruct((part, emb), F32),
-            jax.ShapeDtypeStruct((per_dev, 1), F32),
+            jax.ShapeDtypeStruct((1, per_dev), F32),
         ),
-        in_specs=[any_spec] * 6,
+        in_specs=[hbm_spec] * 6,
         out_specs=(vmem_spec,) * 3,
         scratch_shapes=[
             vmem((per_dev, emb), F32),
-            vmem((per_dev, probes), F32),
-            vmem((per_dev, probes), I32),
-            vmem((per_dev, probes), I32),
+            vmem((probes, per_dev), F32),
+            vmem((probes, per_dev), I32),
+            vmem((probes, per_dev), I32),
             vmem((pass_dev, emb), F32),
             vmem(list_sizes.shape, I32),
             vmem((chunks, 1, width), F32),
@@ -429,14 +472,21 @@
             dma,
             dma,
             dma,
-            dma,
-            dma,
+            dma((groups,)),
+            dma((groups,)),
         ],
         compiler_params=pltpu.CompilerParams(
-            collective_id=0, has_side_effects=True, vmem_limit_bytes=40 * 1024 * 1024
+            collective_id=0, has_side_effects=True, vmem_limit_bytes=60 * 1024 * 1024
         ),
-    )(queries, reader_logits, probe_shards, probe_within, passages, list_sizes)
-    return qg, pg, loss[:, 0]
+    )(queries, reader_logits.T, probe_shards.T, probe_within.T, passages, list_sizes)
+    qg, pg, loss = pl.pallas_call(
+        store,
+        out_shape=tuple(jax.ShapeDtypeStruct(x.shape, F32) for x in (qg, pg, loss)),
+        in_specs=[vmem_spec] * 3,
+        out_specs=(hbm_spec,) * 3,
+        scratch_shapes=[dma((3,))],
+    )(qg, pg, loss)
+    return qg, pg, loss.reshape(per_dev)
 
 
 def solution(mesh):

time: 63.7 us -> 55.8 us (0.88)
  local copies, waits for them, and re-layouts: 4.42 us -> 0 us
  Pallas kernels: 57.7 us -> 55 us
    unnamed x15 -> x0, local copies, waits for them, and re-layouts: 4.42 us -> none
    pallas_call x1, Pallas kernels: 57.7 us -> 53.6 us  [local(): pl.pallas_call(functools.partial(kernel, shards, groups, cap), out_shape=...]
    pallas_call x0 -> x1, Pallas kernels: none -> 1.45 us  [local(): pl.pallas_call(store, out_shape=tuple((jax.ShapeDtypeStruct(x.shape, F32)...]
where the time goes in v2:
time: 55.8 us; the launch traced here: 55.7 us
  Pallas kernels  55 us (99%)
  between operations  0.64 us (1%)
    pallas_call x1, Pallas kernels, local(): pl.pallas_call(functools.partial(kernel, shards, groups, cap), out_shape=...  53.6 us
    pallas_call x1, Pallas kernels, local(): pl.pallas_call(store, out_shape=tuple((jax.ShapeDtypeStruct(x.shape, F32)...  1.45 us

profile of v2, /device:TPU:1, one launch (start us, length us, event | category | flops | bytes accessed | tf_op | source)
XLA Modules:
  0.0 55.7 jit_solution(1312665667705718594)
XLA Ops:
  0.6 53.6 %shard_map.85 = (f32[32,128]{1,0:T(8,128)}, f32[96,128]{1,0:T(8,128)}, f32[1,32]{1,0:T(1,128)}) custom-call(f32[32,128]{1,0:T(8,128)} %q_hbm.1, f32[16,32]{1,0:T(8,128)} %bitcast.4, s32[16,32]{1,0:T(8,128)} %bitcast.5, s32[16,32]{1,0:T(8,128)} %bitcast.6, f32[768,128]{1,0:T(8,128)} %p_hbm.1, s32[1,8]{1,0:T(1,128)} %ls_hbm.1), custom_call_target="tpu_custom_call" | custom-call | tf_op jit(solution)/shard_map/pallas_call | solution.py:425
  54.2 1.4 %shard_map.86 = (f32[32,128]{1,0:T(8,128)}, f32[96,128]{1,0:T(8,128)}, f32[1,32]{1,0:T(1,128)}) custom-call(f32[32,128]{1,0:T(8,128)} %get-tuple-element.9.qg_ref, f32[96,128]{1,0:T(8,128)} %get-tuple-element.10.pg_ref, f32[1,32]{1,0:T(1,128)} %get-tuple-element.11.loss_ref), custom_call_target="tpu_custom_call" | custom-call | tf_op jit(solution)/shard_map/pallas_call | solution.py:482

commit v3 on v2

--- a/solution.py
+++ b/solution.py
@@ -58,10 +58,7 @@
     pw_v,
     p_v,
     ls_v,
-    meta_s,
-    meta_r,
-    rows_s,
-    rows_r,
+    blk,
     stat_s,
     stat_r,
     coef_s,
@@ -77,15 +74,25 @@
     pcat,
     ptr,
     owner,
+    rank_of,
+    same_of,
+    want,
+    wide,
+    rows_s,
+    rows_f,
+    ident_s,
+    ident,
     eh,
     el,
     rch,
     rcm,
     in_sem,
-    meta_ss,
-    meta_rs,
+    y_ss,
+    y_rs,
     rows_ss,
     rows_rs,
+    ident_ss,
+    ident_rs,
     stat_ss,
     stat_rs,
     coef_ss,
@@ -102,15 +109,24 @@
     chunks = shards // GROUP
     width = GROUP * cap
     slots = shards * cap
+    lists_dev = ls_v.shape[1]
     scale = 1.0 / math.sqrt(emb)
     me = lax.axis_index("lists")
     qb = lax.axis_index("qb")
 
-    def peer(j):
-        return {"lists": lax.rem(me + j, shards)}
-
-    def source(j):
-        return {"lists": lax.rem(me - j + shards, shards)}
+    nc, ny = 2, 8
+    nx = shards // (nc * ny)
+    x, y, core = me // (ny * nc), lax.rem(me // nc, ny), lax.rem(me, nc)
+
+    def away(dx, dy, dc):
+        there = lax.rem(x + dx, nx) * ny + lax.rem(y + dy, ny)
+        return {"lists": there * nc + lax.rem(core + dc, nc)}
+
+    def peer(c, dy):
+        return away(c // nc, dy, c % nc)
+
+    def source(c, dy):
+        return away(nx - c // nc, ny - dy, c % nc)
 
     def to(src, dst, ss, rs, device):
         return pltpu.make_async_remote_copy(
@@ -132,69 +148,32 @@
 
     barrier = pltpu.get_barrier_semaphore()
 
-    def greet(j, carry):
-        pl.semaphore_signal(barrier, inc=1, device_id=peer(j), device_id_type=MESH)
-        return carry
-
-    lax.fori_loop(1, shards, greet, 0)
-    for d in range(1, groups):
-        pl.semaphore_signal(
-            barrier, inc=1, device_id={"qb": lax.rem(qb + d, groups)}, device_id_type=MESH
-        )
-
-    expand[...] = (
-        lax.broadcasted_iota(I32, (shards, slots), 1) // cap
-        == lax.broadcasted_iota(I32, (shards, slots), 0)
-    ).astype(BF16)
-    place = (lax.rem(lax.broadcasted_iota(I32, (per_dev, slots), 1), cap) + 1).astype(F32)
-    tri = (
-        lax.broadcasted_iota(I32, (per_dev, per_dev), 1)
-        <= lax.broadcasted_iota(I32, (per_dev, per_dev), 0)
-    ).astype(BF16)
-    shard_lane = lax.broadcasted_iota(I32, (per_dev, shards), 1)
+    greeted = [away(0, dy, 0) for dy in (4, 3, 5, 2, 6, 1, 7)]
+    greeted += [away(c // nc, 0, c % nc) for c in (4, 5, 2, 6, 3, 7, 1)]
+    greeted += [{"qb": lax.rem(qb + d, groups)} for d in (2, groups - 2, 1, groups - 1)]
+    for device in greeted:
+        pl.semaphore_signal(barrier, inc=1, device_id=device, device_id_type=MESH)
+
     for load in loads[:3]:
         load.wait()
     ps = ps_v[...]
-    rel = jnp.where(ps >= me, ps - me, ps - me + shards).T
-    within = pw_v[...].T + 1
-    w1 = jnp.zeros((per_dev, shards), I32)
-    for k in range(probes):
-        w1 = jnp.where(rel[:, k : k + 1] == shard_lane, within[:, k : k + 1], w1)
-    w1 = w1.astype(F32)
-    hot = w1 > 0.0
-    rank = mm(tri, hot.astype(BF16))
-    slot1 = jnp.where(hot, rank, 0.0)
-    both = mm(jnp.concatenate([slot1, w1], axis=0).astype(BF16), expand[...])
-    mask = both[:per_dev] == place
-    disp[...] = mask.astype(F32)
-    ids = jnp.sum(jnp.where(mask, both[per_dev:], 0.0), axis=0, keepdims=True)
-    for c in range(chunks):
-        meta_s[c] = ids[:, c * width : (c + 1) * width]
-    q_scaled = q_v[...] * scale
-    q3 = jnp.concatenate(split3(q_scaled), axis=0)
-    for c in range(chunks):
-        d1 = disp[:, c * width : (c + 1) * width].astype(BF16)
-        block = mm_tn(jnp.concatenate([d1, d1, d1], axis=0), q3)
-        rows_s[pl.ds(c * GROUP, GROUP)] = block.reshape(GROUP, cap, emb)
-
-    pl.semaphore_wait(barrier, shards - 1 + groups - 1)
-
-    def send_meta(j, carry):
-        c = j // GROUP
-        to(meta_s.at[c], meta_r.at[j], meta_ss, meta_rs.at[c], peer(j)).start()
-        return carry
-
-    def send_rows(j, carry):
-        c = j // GROUP
-        to(rows_s.at[j], rows_r.at[j], rows_ss, rows_rs.at[c], peer(j)).start()
-        return carry
-
-    def send_both(j, carry):
-        return send_rows(j, send_meta(j, carry))
-
-    lax.fori_loop(1, shards, send_both, 0)
-    meta_r[0] = meta_s[0]
-    rows_r[0] = rows_s[0]
+    code = (ps * lists_dev + pw_v[...]).astype(F32)
+    blk[0, 0:per_dev, :] = q_v[...] * scale
+    quarter = probes // 4
+    blk[0, per_dev : per_dev + quarter, :] = jnp.concatenate(
+        [code[i * quarter : (i + 1) * quarter] for i in range(4)], axis=1
+    )
+    used = pl.ds(0, per_dev + quarter)
+
+    def block(j):
+        return blk.at[j].at[used]
+
+    def blocks(j, n):
+        return blk.at[pl.ds(j, n), used]
+
+    pl.semaphore_wait(barrier, len(greeted))
+    for dy in (4, 3, 5, 2, 6, 1, 7):
+        to(block(0), block(dy), y_ss, y_rs.at[dy], away(0, dy, 0)).start()
 
     for load in loads[3:]:
         load.wait()
@@ -215,12 +194,83 @@
             own = own + jnp.where(number >= end, 1.0, 0.0)
         owner[i * part : (i + 1) * part, :] = own
 
+    lane_q = lax.rem(lax.broadcasted_iota(I32, (4 * per_dev, GROUP * per_dev), 0), per_dev)
+    wide_q = lax.rem(lax.broadcasted_iota(I32, (4 * per_dev, GROUP * per_dev), 1), per_dev)
+    rank_of[...] = (lane_q <= wide_q).astype(BF16)
+    same_of[...] = (lane_q == wide_q).astype(BF16)
+    slot_at = lax.broadcasted_iota(I32, (width, GROUP * per_dev), 0)
+    lane_at = lax.broadcasted_iota(I32, (width, GROUP * per_dev), 1)
+    want[...] = jnp.where(
+        lane_at // per_dev == slot_at // cap, lax.rem(slot_at, cap) + 1, -1
+    ).astype(F32)
+
+    diagonal = (
+        lax.broadcasted_iota(I32, (GROUP, GROUP * per_dev), 1) // per_dev
+        == lax.broadcasted_iota(I32, (GROUP, GROUP * per_dev), 0)
+    )
+    used_row = lax.broadcasted_iota(I32, (GROUP, 8, emb), 1) < quarter
+
+    for dy in (1, 7, 2, 6, 3, 5, 4):
+        to(block(dy), block(dy), y_ss, y_rs.at[dy], away(0, dy, 0)).wait_recv()
+    wide[...] = jnp.concatenate(
+        split3(blk[0:ny, 0:per_dev, :].reshape(ny * per_dev, emb)), axis=1
+    )
+
+    def compact(c, rows_out, ident_out):
+        taker = away(c // nc, 0, c % nc)["lists"]
+        number = blk[0:ny, per_dev : per_dev + 8, :] - (taker * lists_dev).astype(F32)
+        found = used_row & (number >= 0.0) & (number < lists_dev)
+        found = jnp.sum(jnp.where(found, number + 1.0, 0.0), axis=1)
+        rank = mm((found > 0.0).astype(BF16), rank_of[...])
+        one = mm(found.astype(BF16), same_of[...])
+        slot = jnp.where(one > 0.0, rank, 0.0)
+        slot = jnp.broadcast_to(slot[:, None, :], (GROUP, cap, GROUP * per_dev))
+        pick = (slot.reshape(width, GROUP * per_dev) == want[...]).astype(BF16)
+        picked = mm(pick, wide[...])
+        hi, mid, low = (picked[:, i * emb : (i + 1) * emb] for i in range(3))
+        rows_out[c] = (hi + mid) + low
+        number = mm_nt(jnp.where(diagonal, one, 0.0).astype(BF16), pick)
+        ident_out[c] = jnp.sum(number, axis=0, keepdims=True)
+
+    def handed(c):
+        taker = away(c // nc, 0, c % nc)
+        return (
+            to(rows_s.at[c], rows_f.at[c], rows_ss, rows_rs.at[c], taker),
+            to(ident_s.at[c], ident.at[c], ident_ss, ident_rs.at[c], taker),
+        )
+
+    for c in (2, 6, 3, 7, 4, 5, 1):
+        compact(c, rows_s, ident_s)
+        for copy in handed(c):
+            copy.start()
+    compact(0, rows_f, ident)
+
+    expand[...] = (
+        lax.broadcasted_iota(I32, (shards, slots), 1) // cap
+        == lax.broadcasted_iota(I32, (shards, slots), 0)
+    ).astype(BF16)
+    place = (lax.rem(lax.broadcasted_iota(I32, (per_dev, slots), 1), cap) + 1).astype(F32)
+    tri = (
+        lax.broadcasted_iota(I32, (per_dev, per_dev), 1)
+        <= lax.broadcasted_iota(I32, (per_dev, per_dev), 0)
+    ).astype(BF16)
+    shard_lane = lax.broadcasted_iota(I32, (per_dev, shards), 1)
+    dx = lax.rem(ps // (ny * nc) - x + nx, nx)
+    dy = lax.rem(lax.rem(ps // nc, ny) - y + ny, ny)
+    dc = lax.rem(lax.rem(ps, nc) - core + nc, nc)
+    rel = ((dx * nc + dc) * ny + dy).T
     lg = lg_v[...]
     lg = lg - jnp.max(lg, axis=0, keepdims=True)
     lt = (lg - jnp.log(jnp.sum(jnp.exp(lg), axis=0, keepdims=True))).T
+    hot = jnp.zeros((per_dev, shards), F32)
     lt_shard = jnp.zeros((per_dev, shards), F32)
     for k in range(probes):
-        lt_shard = jnp.where(rel[:, k : k + 1] == shard_lane, lt[:, k : k + 1], lt_shard)
+        here = rel[:, k : k + 1] == shard_lane
+        hot = jnp.where(here, 1.0, hot)
+        lt_shard = jnp.where(here, lt[:, k : k + 1], lt_shard)
+    slot1 = jnp.where(hot > 0.0, mm(tri, hot.astype(BF16)), 0.0)
+    spread = mm(slot1.astype(BF16), expand[...])
+    disp[...] = (spread == place).astype(F32)
     lt3 = mm(jnp.concatenate(split3(lt_shard), axis=0), expand[...])
     logt[...] = lt3[:per_dev] + lt3[per_dev : 2 * per_dev] + lt3[2 * per_dev :]
 
@@ -232,58 +282,73 @@
             out = jnp.where(lane == jj, ref[c * GROUP + jj, row : row + 1, :], out)
         return out
 
-    def wait_chunk(ref, sems, c):
-        @pl.when(c == 0)
+    def forward(dx, carry):
+        at = pl.ds(pl.multiple_of(dx * nc * width, nc * width), nc * width)
+
+        @pl.when(dx > 0)
         def _():
-            view = ref.at[pl.ds(1, GROUP - 1)]
-            to(view, view, rows_ss, sems.at[0], peer(1)).wait_recv()
-
-        @pl.when(c > 0)
-        def _():
-            view = ref.at[pl.ds(c * GROUP, GROUP)]
-            to(view, view, rows_ss, sems.at[c], peer(1)).wait_recv()
-
-    def forward(c, carry):
-        wait_chunk(meta_r, meta_rs, c)
-        ident = gather_row(meta_r, c, 0)
-        wait_chunk(rows_r, rows_rs, c)
-        rows = rows_r[pl.ds(c * GROUP, GROUP)].reshape(width, emb)
-        rh, rm, rl = split3(rows)
-        score = mm_nt(pcat[...], jnp.concatenate([rh, rh, rm, rh, rl, rm], axis=1))
-        score = jnp.where(owner[...] == ident, score, LOW)
+            for copy in handed(nc * dx):
+                copy.wait_recv()
+
+        for copy in handed(nc * dx + 1):
+            copy.wait_recv()
+        hi, mid, low = split3(rows_f[pl.ds(nc * dx, nc)].reshape(nc * width, emb))
+        score = mm_nt(pcat[...], jnp.concatenate([hi, hi, mid, hi, low, mid], axis=1))
+        number = jnp.concatenate([ident[nc * dx], ident[nc * dx + 1]], axis=1)
+        held = jnp.concatenate([owner[...]] * nc, axis=1)
+        score = jnp.where(held == number, score, LOW)
         top = jnp.max(score, axis=0, keepdims=True)
         expo = jnp.exp(score - top)
         norm = jnp.sum(expo, axis=0, keepdims=True)
-        stat_s[c, 0:1, :] = top
-        stat_s[c, 1:2, :] = norm
-
-        def send_stat(jj, carry):
-            j = c * GROUP + jj
-            to(stat_s.at[c], stat_r.at[j], stat_ss, stat_rs, source(j)).start()
-            return carry
-
-        lax.fori_loop(jnp.where(c == 0, 1, 0), GROUP, send_stat, 0)
+        for k in range(nc):
+            c = nc * dx + k
+            stat_s[c, 0:1, :] = top[:, k * width : (k + 1) * width]
+            stat_s[c, 1:2, :] = norm[:, k * width : (k + 1) * width]
+        for k in range(nc):
+            c = nc * dx + k
+            send_chunk(c, lambda j: stat_s.at[c], stat_r, stat_ss, stat_rs, source)
         hi, lo = split2(expo)
-        at = pl.ds(pl.multiple_of(c * width, width), width)
         eh[:, at] = hi
         el[:, at] = lo
         return carry
 
-    lax.fori_loop(0, chunks, forward, 0)
+    def send_chunk(c, src, dst, ss, rs, device):
+        for dy in (4, 3, 5, 2, 6, 1, 7, 0):
+            j = c * ny + dy
+            if dy:
+                to(src(j), dst.at[j], ss, rs, device(c, dy)).start()
+            else:
+
+                @pl.when(c > 0)
+                def _():
+                    to(src(j), dst.at[j], ss, rs, device(c, 0)).start()
+
+    def send_all(src, dst, ss, rs, device):
+        def one(i, carry):
+            c = lax.rem(i + chunks // 2, chunks)
+            send_chunk(c, lambda j: src(c, j), dst, ss, rs, device)
+            return carry
+
+        lax.fori_loop(0, chunks, one, 0)
+
+    def in_turn(i, carry):
+        return forward(jnp.where(i < 2, i, 5 - i), carry)
+
+    lax.fori_loop(0, nx, in_turn, 0)
     stat_r[0] = stat_s[0]
 
-    def query_part(c, carry):
-        at = pl.ds(pl.multiple_of(c * width, width), width)
+    def query_part(i, carry):
+        at = pl.ds(pl.multiple_of(i * nc * width, nc * width), nc * width)
         hi, lo = eh[:, at], el[:, at]
         part_t = mm(ptr[:, :pass_dev], hi) + mm(ptr[:, :pass_dev], lo) + mm(ptr[:, pass_dev:], hi)
-        u_s[pl.ds(c * GROUP, GROUP)] = part_t.T.reshape(GROUP, cap, emb)
+        u_s[pl.ds(i * nc * GROUP, nc * GROUP)] = part_t.T.reshape(nc * GROUP, cap, emb)
         return carry
 
-    lax.fori_loop(0, chunks, query_part, 0)
+    lax.fori_loop(0, nx, query_part, 0)
     u_r[0] = u_s[0]
 
     rest = stat_r.at[pl.ds(1, shards - 1)]
-    to(rest, rest, stat_ss, stat_rs, peer(1)).wait_recv()
+    to(rest, rest, stat_ss, stat_rs, away(0, 0, 1)).wait_recv()
     top = jnp.concatenate([gather_row(stat_r, c, 0) for c in range(chunks)], axis=1)
     norm = jnp.concatenate([gather_row(stat_r, c, 1) for c in range(chunks)], axis=1)
     mask = disp[...] > 0.0
@@ -299,18 +364,9 @@
     for c in range(chunks):
         coef_s[c] = coef_row[:, c * width : (c + 1) * width]
 
-    def send_coef(j, carry):
-        to(coef_s.at[j // GROUP], coef_r.at[j], coef_ss, coef_rs, peer(j)).start()
-        return carry
-
-    lax.fori_loop(1, shards, send_coef, 0)
+    send_all(lambda c, j: coef_s.at[c], coef_r, coef_ss, coef_rs, peer)
     coef_r[0] = coef_s[0]
-
-    def send_u(j, carry):
-        to(u_s.at[j], u_r.at[j], u_ss, u_rs, source(j)).start()
-        return carry
-
-    lax.fori_loop(1, shards, send_u, 0)
+    send_all(lambda c, j: u_s.at[j], u_r, u_ss, u_rs, source)
     acoef[...] = coef * scale
     log_share = jnp.log(norm) + gap - jnp.log(total)
     term = jnp.where(mask, target * (log_target - log_share), 0.0)
@@ -322,11 +378,10 @@
     )
 
     rest = coef_r.at[pl.ds(1, shards - 1)]
-    to(rest, rest, coef_ss, coef_rs, peer(1)).wait_recv()
+    to(rest, rest, coef_ss, coef_rs, away(0, 0, 1)).wait_recv()
     for c in range(chunks):
         column = jnp.broadcast_to(gather_row(coef_r, c, 0), (width, width)).T
-        rows = rows_r[c * GROUP : (c + 1) * GROUP].reshape(width, emb)
-        hi, mid = split2(rows * column)
+        hi, mid = split2(rows_f[c] * column)
         rch[c * width : (c + 1) * width, :] = hi
         rcm[c * width : (c + 1) * width, :] = mid
     rc = jnp.concatenate([rch[...], rcm[...]], axis=1)
@@ -373,7 +428,7 @@
     direct[3].start()
 
     rest = u_r.at[pl.ds(1, shards - 1)]
-    to(rest, rest, u_ss, u_rs, peer(1)).wait_recv()
+    to(rest, rest, u_ss, u_rs, away(0, 0, 1)).wait_recv()
     qg = jnp.zeros((per_dev, emb), F32)
     for c in range(chunks):
         ah, am = split2(acoef[:, c * width : (c + 1) * width])
@@ -387,15 +442,15 @@
         out = out + z_r[4 + slot]
     pg_ref[...] = out
 
-    for ref, sem in (
-        (meta_r, meta_ss),
-        (rows_r, rows_ss),
-        (stat_r, stat_ss),
-        (coef_r, coef_ss),
-        (u_r, u_ss),
+    for view, sem in (
+        (blocks(1, ny - 1), y_ss),
+        (rows_f.at[pl.ds(1, chunks - 1)], rows_ss),
+        (ident.at[pl.ds(1, chunks - 1)], ident_ss),
+        (stat_r.at[pl.ds(1, shards - 1)], stat_ss),
+        (coef_r.at[pl.ds(1, shards - 1)], coef_ss),
+        (u_r.at[pl.ds(1, shards - 1)], u_ss),
     ):
-        rest = ref.at[pl.ds(1, shards - 1)]
-        to(rest, rest, sem, coef_rs, peer(1)).wait_send()
+        to(view, view, sem, coef_rs, away(0, 0, 1)).wait_send()
     for copy in relays + direct:
         copy.wait_send()
 
@@ -438,10 +493,7 @@
             vmem((probes, per_dev), I32),
             vmem((pass_dev, emb), F32),
             vmem(list_sizes.shape, I32),
-            vmem((chunks, 1, width), F32),
-            vmem((shards, 1, width), F32),
-            vmem((shards, cap, emb), F32),
-            vmem((shards, cap, emb), F32),
+            vmem((8, per_dev + 8, emb), F32),
             vmem((chunks, 2, width), F32),
             vmem((shards, 2, width), F32),
             vmem((chunks, 1, width), F32),
@@ -457,15 +509,25 @@
             vmem((pass_dev, 6 * emb), BF16),
             vmem((emb, 2 * pass_dev), BF16),
             vmem((pass_dev, width), F32),
+            vmem((4 * per_dev, GROUP * per_dev), BF16),
+            vmem((4 * per_dev, GROUP * per_dev), BF16),
+            vmem((width, GROUP * per_dev), F32),
+            vmem((GROUP * per_dev, 3 * emb), BF16),
+            vmem((chunks, width, emb), F32),
+            vmem((chunks, width, emb), F32),
+            vmem((chunks, 1, width), F32),
+            vmem((chunks, 1, width), F32),
             vmem((pass_dev, slots), BF16),
             vmem((pass_dev, slots), BF16),
             vmem((slots, emb), BF16),
             vmem((slots, emb), BF16),
             dma((5 + groups,)),
             dma,
-            dma((chunks,)),
-            dma,
-            dma((chunks,)),
+            dma((8,)),
+            dma,
+            dma((8,)),
+            dma,
+            dma((8,)),
             dma,
             dma,
             dma,

time: 55.8 us -> 53.1 us (0.952)
  Pallas kernels: 55 us -> 52.1 us
    pallas_call x1, Pallas kernels: 53.6 us -> 50.6 us  [local(): pl.pallas_call(functools.partial(kernel, shards, groups, cap), out_shape=...]
where the time goes in v3:
time: 53.1 us; the launch traced here: 52.7 us
  Pallas kernels  52.1 us (98%)
  between operations  0.64 us (1%)
    pallas_call x1, Pallas kernels, local(): pl.pallas_call(functools.partial(kernel, shards, groups, cap), out_shape=...  50.6 us
    pallas_call x1, Pallas kernels, local(): pl.pallas_call(store, out_shape=tuple((jax.ShapeDtypeStruct(x.shape, F32)...  1.45 us

profile of v3, /device:TPU:1, one launch (start us, length us, event | category | flops | bytes accessed | tf_op | source)
XLA Modules:
  0.0 52.7 jit_solution(3718646017612709812)
XLA Ops:
  0.6 50.6 %shard_map.85 = (f32[32,128]{1,0:T(8,128)}, f32[96,128]{1,0:T(8,128)}, f32[1,32]{1,0:T(1,128)}) custom-call(f32[32,128]{1,0:T(8,128)} %q_hbm.1, f32[16,32]{1,0:T(8,128)} %bitcast.4, s32[16,32]{1,0:T(8,128)} %bitcast.5, s32[16,32]{1,0:T(8,128)} %bitcast.6, f32[768,128]{1,0:T(8,128)} %p_hbm.1, s32[1,8]{1,0:T(1,128)} %ls_hbm.1), custom_call_target="tpu_custom_call" | custom-call | tf_op jit(solution)/shard_map/pallas_call | solution.py:480
  51.3 1.4 %shard_map.86 = (f32[32,128]{1,0:T(8,128)}, f32[96,128]{1,0:T(8,128)}, f32[1,32]{1,0:T(1,128)}) custom-call(f32[32,128]{1,0:T(8,128)} %get-tuple-element.9.qg_ref, f32[96,128]{1,0:T(8,128)} %get-tuple-element.10.pg_ref, f32[1,32]{1,0:T(1,128)} %get-tuple-element.11.loss_ref), custom_call_target="tpu_custom_call" | custom-call | tf_op jit(solution)/shard_map/pallas_call | solution.py:544

commit v4 on v3

--- a/solution.py
+++ b/solution.py
@@ -49,6 +49,9 @@
     pw_hbm,
     p_hbm,
     ls_hbm,
+    qg_hbm,
+    pg_hbm,
+    loss_hbm,
     qg_ref,
     pg_ref,
     loss_ref,
@@ -87,6 +90,7 @@
     rch,
     rcm,
     in_sem,
+    out_sem,
     y_ss,
     y_rs,
     rows_ss,
@@ -133,7 +137,15 @@
             src_ref=src, dst_ref=dst, send_sem=ss, recv_sem=rs, device_id=device, device_id_type=MESH
         )
 
-    order = [3, 5, 4, 2, 6, 1, 7, 0]
+    barrier = pltpu.get_barrier_semaphore()
+
+    greeted = [{"qb": lax.rem(qb + d, groups)} for d in (2, groups - 2, 1, groups - 1)]
+    greeted += [away(0, dy, 0) for dy in (4, 3, 5, 2, 6, 1, 7)]
+    greeted += [away(c // nc, 0, c % nc) for c in (4, 5, 2, 6, 3, 7, 1)]
+    for device in greeted:
+        pl.semaphore_signal(barrier, inc=1, device_id=device, device_id_type=MESH)
+
+    order = [4, 3, 5, 2, 6, 1, 7, 0]
     small = [(q_hbm, q_v), (ps_hbm, ps_v), (pw_hbm, pw_v), (lg_hbm, lg_v), (ls_hbm, ls_v)]
     loads = [pltpu.make_async_copy(a, b, in_sem.at[i]) for i, (a, b) in enumerate(small)]
     for i, d in enumerate(order):
@@ -145,14 +157,6 @@
         )
     for load in loads:
         load.start()
-
-    barrier = pltpu.get_barrier_semaphore()
-
-    greeted = [away(0, dy, 0) for dy in (4, 3, 5, 2, 6, 1, 7)]
-    greeted += [away(c // nc, 0, c % nc) for c in (4, 5, 2, 6, 3, 7, 1)]
-    greeted += [{"qb": lax.rem(qb + d, groups)} for d in (2, groups - 2, 1, groups - 1)]
-    for device in greeted:
-        pl.semaphore_signal(barrier, inc=1, device_id=device, device_id_type=MESH)
 
     for load in loads[:3]:
         load.wait()
@@ -216,20 +220,26 @@
         split3(blk[0:ny, 0:per_dev, :].reshape(ny * per_dev, emb)), axis=1
     )
 
+    codes = blk[0:ny, per_dev : per_dev + 8, :]
+    found = []
+    for c in range(chunks):
+        taker = away(c // nc, 0, c % nc)["lists"]
+        number = codes - (taker * lists_dev).astype(F32)
+        here = used_row & (number >= 0.0) & (number < lists_dev)
+        found.append(jnp.sum(jnp.where(here, number + 1.0, 0.0), axis=1))
+    found = jnp.concatenate(found, axis=0)
+    rank = mm((found > 0.0).astype(BF16), rank_of[...])
+    one = mm(found.astype(BF16), same_of[...])
+    slot = jnp.where(one > 0.0, rank, 0.0)
+
     def compact(c, rows_out, ident_out):
-        taker = away(c // nc, 0, c % nc)["lists"]
-        number = blk[0:ny, per_dev : per_dev + 8, :] - (taker * lists_dev).astype(F32)
-        found = used_row & (number >= 0.0) & (number < lists_dev)
-        found = jnp.sum(jnp.where(found, number + 1.0, 0.0), axis=1)
-        rank = mm((found > 0.0).astype(BF16), rank_of[...])
-        one = mm(found.astype(BF16), same_of[...])
-        slot = jnp.where(one > 0.0, rank, 0.0)
-        slot = jnp.broadcast_to(slot[:, None, :], (GROUP, cap, GROUP * per_dev))
-        pick = (slot.reshape(width, GROUP * per_dev) == want[...]).astype(BF16)
+        mine = slice(c * GROUP, (c + 1) * GROUP)
+        wanted = jnp.broadcast_to(slot[mine][:, None, :], (GROUP, cap, GROUP * per_dev))
+        pick = (wanted.reshape(width, GROUP * per_dev) == want[...]).astype(BF16)
         picked = mm(pick, wide[...])
         hi, mid, low = (picked[:, i * emb : (i + 1) * emb] for i in range(3))
         rows_out[c] = (hi + mid) + low
-        number = mm_nt(jnp.where(diagonal, one, 0.0).astype(BF16), pick)
+        number = mm_nt(jnp.where(diagonal, one[mine], 0.0).astype(BF16), pick)
         ident_out[c] = jnp.sum(number, axis=0, keepdims=True)
 
     def handed(c):
@@ -239,10 +249,12 @@
             to(ident_s.at[c], ident.at[c], ident_ss, ident_rs.at[c], taker),
         )
 
-    for c in (2, 6, 3, 7, 4, 5, 1):
-        compact(c, rows_s, ident_s)
-        for copy in handed(c):
-            copy.start()
+    for pair in ((2, 6), (3, 7), (4, 5), (1,)):
+        for c in pair:
+            compact(c, rows_s, ident_s)
+        for c in pair:
+            for copy in handed(c):
+                copy.start()
     compact(0, rows_f, ident)
 
     expand[...] = (
@@ -376,6 +388,8 @@
     loss_ref[...] = jnp.sum(
         jnp.where(diagonal, jnp.sum(term, axis=1, keepdims=True), 0.0), axis=0, keepdims=True
     )
+    stores = [pltpu.make_async_copy(loss_ref, loss_hbm, out_sem.at[0])]
+    stores[0].start()
 
     rest = coef_r.at[pl.ds(1, shards - 1)]
     to(rest, rest, coef_ss, coef_rs, away(0, 0, 1)).wait_recv()
@@ -386,11 +400,11 @@
         rcm[c * width : (c + 1) * width, :] = mid
     rc = jnp.concatenate([rch[...], rcm[...]], axis=1)
 
-    def passage_part(h):
-        rows_at = slice(h * part, (h + groups // 2) * part)
+    def passage_part(h, n):
+        rows_at = slice(h * part, (h + n) * part)
         both = mm(eh[rows_at, :], rc) + mm(el[rows_at, :], rc)
         block = both[:, :emb] + both[:, emb:]
-        for i in range(groups // 2):
+        for i in range(n):
             z_s[order[h + i]] = block[i * part : (i + 1) * part]
 
     half = part // 2
@@ -401,16 +415,18 @@
         return to(src, z_r.at[slot].at[rows_at], z_ss.at[slot], z_rs.at[slot], device)
 
     every = pl.ds(0, part)
-    passage_part(0)
     relays = [
         hop(z_s.at[3], 0, every, 1),
         hop(z_s.at[5], 1, every, -1),
         hop(z_s.at[4].at[first], 2, first, 2),
         hop(z_s.at[4].at[second], 3, second, -2),
     ]
-    for copy in relays:
-        copy.start()
-    passage_part(groups // 2)
+    passage_part(0, 2)
+    for i in (2, 3, 0):
+        relays[i].start()
+    passage_part(2, 2)
+    relays[1].start()
+    passage_part(4, 4)
     direct = [hop(z_s.at[1], 4, every, 1), hop(z_s.at[7], 5, every, -1)]
     for copy in direct:
         copy.start()
@@ -435,12 +451,16 @@
         uh, um = split2(u_r[c * GROUP : (c + 1) * GROUP].reshape(width, emb))
         qg = qg + mm(ah, uh) + mm(am, uh) + mm(ah, um)
     qg_ref[...] = qg
+    stores.append(pltpu.make_async_copy(qg_ref, qg_hbm, out_sem.at[1]))
+    stores[1].start()
 
     out = z_s[0]
     for slot, copy in enumerate(direct):
         copy.wait_recv()
         out = out + z_r[4 + slot]
     pg_ref[...] = out
+    stores.append(pltpu.make_async_copy(pg_ref, pg_hbm, out_sem.at[2]))
+    stores[2].start()
 
     for view, sem in (
         (blocks(1, ny - 1), y_ss),
@@ -453,6 +473,8 @@
         to(view, view, sem, coef_rs, away(0, 0, 1)).wait_send()
     for copy in relays + direct:
         copy.wait_send()
+    for copy in stores:
+        copy.wait()
 
 
 def store(qg_ref, pg_ref, loss_ref, qg_out, pg_out, loss_out, sems):
@@ -485,8 +507,11 @@
             jax.ShapeDtypeStruct((1, per_dev), F32),
         ),
         in_specs=[hbm_spec] * 6,
-        out_specs=(vmem_spec,) * 3,
+        out_specs=(hbm_spec,) * 3,
         scratch_shapes=[
+            vmem((per_dev, emb), F32),
+            vmem((part, emb), F32),
+            vmem((1, per_dev), F32),
             vmem((per_dev, emb), F32),
             vmem((probes, per_dev), F32),
             vmem((probes, per_dev), I32),
@@ -522,6 +547,7 @@
             vmem((slots, emb), BF16),
             vmem((slots, emb), BF16),
             dma((5 + groups,)),
+            dma((3,)),
             dma,
             dma((8,)),
             dma,

time: 53.1 us -> 52.5 us (0.989)
  no operation moved by 1% of the time
where the time goes in v4:
time: 52.5 us; the launch traced here: 52.3 us
  Pallas kernels  51.7 us (98%)
  between operations  0.64 us (1%)
    pallas_call x1, Pallas kernels, local(): pl.pallas_call(functools.partial(kernel, shards, groups, cap), out_shape=...  50.2 us
    pallas_call x1, Pallas kernels, local(): pl.pallas_call(store, out_shape=tuple((jax.ShapeDtypeStruct(x.shape, F32)...  1.45 us

profile of v4, /device:TPU:1, one launch (start us, length us, event | category | flops | bytes accessed | tf_op | source)
XLA Modules:
  0.0 52.3 jit_solution(11838024374762950465)
XLA Ops:
  0.6 50.2 %shard_map.85 = (f32[32,128]{1,0:T(8,128)}, f32[96,128]{1,0:T(8,128)}, f32[1,32]{1,0:T(1,128)}) custom-call(f32[32,128]{1,0:T(8,128)} %q_hbm.1, f32[16,32]{1,0:T(8,128)} %bitcast.4, s32[16,32]{1,0:T(8,128)} %bitcast.5, s32[16,32]{1,0:T(8,128)} %bitcast.6, f32[768,128]{1,0:T(8,128)} %p_hbm.1, s32[1,8]{1,0:T(1,128)} %ls_hbm.1), custom_call_target="tpu_custom_call" | custom-call | tf_op jit(solution)/shard_map/pallas_call | solution.py:502
  50.8 1.4 %shard_map.86 = (f32[32,128]{1,0:T(8,128)}, f32[96,128]{1,0:T(8,128)}, f32[1,32]{1,0:T(1,128)}) custom-call(f32[32,128]{1,0:T(8,128)} %get-tuple-element.9.qg_ref, f32[96,128]{1,0:T(8,128)} %get-tuple-element.10.pg_ref, f32[1,32]{1,0:T(1,128)} %get-tuple-element.11.loss_ref), custom_call_target="tpu_custom_call" | custom-call | tf_op jit(solution)/shard_map/pallas_call | solution.py:570
